TPU v7x, 32 devices: a whole 2x2x4 slice. The times are simulated.
32 devices in a mesh: kocc: 8 (over z, y), vrow: 4 (over x, core).
Axes of the slice: x: 2, y: 2, z: 4, core: 2. Of those that a mesh axis runs over, the one named last changes fastest.
Arguments:
- factors: bfloat16 [8, 16, 128, 1536], P('kocc', None, 'vrow'), may hold values from -0.1875 to 0.1875
- amps: bfloat16 [4, 8, 16, 128, 1024], P(None, 'kocc', None, None, 'vrow'), may hold values from -6 to 6
- eps_occ: float32 [8, 16], P('kocc'), may hold values from -1 to -0.3
- eps_vir: bfloat16 [8, 128], P('kocc'), may hold values from 0.099609375 to 1
- col_energy: float32 [1024], P('vrow'), may hold values from 0.2 to 1.5
- q_index: int32 [1], replicated, may hold values from 1 to 7
Outputs:
- sigma: bfloat16 [4, 8, 16, 128, 1024], P(None, 'kocc', None, None, 'vrow')
All inputs are finite; a program needn't handle non-finite values.
Results may differ from a plain program's by a relative error of at most 0.015.
Values may be sent and summed in bfloat16 or wider, within the bound.
A program may use at most 128 MiB of HBM per device.

v0:
```python
import jax
import jax.numpy as jnp
from jax import lax
from jax.sharding import PartitionSpec as P


def from_behind(block, axis, distance):
    devices = range(lax.axis_size(axis))
    route = [((i - distance) % len(devices), i) for i in devices]
    return lax.ppermute(block, axis, route)


def shards(factors, amps, eps_occ, eps_vir, col_energy, q_index):
    kcount = lax.axis_size("kocc")
    shifted, vir_shift = (factors, eps_vir)
    for level in range((kcount - 1).bit_length()):
        arrived = from_behind((shifted, vir_shift), "kocc", 1 << level)
        chosen = q_index[0] // (1 << level) % 2 == 1
        shifted = jnp.where(chosen, arrived[0], shifted)
        vir_shift = jnp.where(chosen, arrived[1], vir_shift)
    amp_local = amps[:, 0]
    cycle_terms = jnp.einsum(
        "iap,riaj->rpj",
        lax.all_gather(shifted, "vrow", axis=2, tiled=True)[0],
        amp_local,
        preferred_element_type=jnp.float32,
    )
    cycle_total = lax.psum(cycle_terms.astype(jnp.bfloat16), "kocc")
    cycle_part = jnp.einsum(
        "iap,rpj->riaj",
        lax.all_gather(shifted, "vrow", axis=2, tiled=True)[0],
        cycle_total,
        preferred_element_type=jnp.float32,
    )
    energy_gap = (
        vir_shift[0].astype(jnp.float32)[None, :, None]
        - eps_occ[0][:, None, None]
        + col_energy[None, None, :]
    )
    sigma_out = (cycle_part + energy_gap[None] * amp_local.astype(jnp.float32)).astype(jnp.bfloat16)
    return sigma_out[:, None]


def solution(mesh):
    in_specs = (
        P("kocc", None, "vrow", None),
        P(None, "kocc", None, None, "vrow"),
        P("kocc", None),
        P("kocc", None),
        P("vrow"),
        P(),
    )
    out_specs = P(None, "kocc", None, None, "vrow")
    return jax.shard_map(shards, mesh=mesh, in_specs=in_specs, out_specs=out_specs, check_vma=False)
```

profile of v0, /device:TPU:0, one launch (start us, length us, event | category | flops | bytes accessed | tf_op | source)
XLA Modules:
  0.0 363.7 jit_solution(8879420228742749629)
XLA Ops:
  6.5 0.0 all-gather.2.cloned.1.call-start
  6.5 3.0 collective-permute-start
  10.2 37.0 %collective-permute-done = bf16[1,16,32,1536]{3,2,1,0:T(8,128)(2,1)S(1)} collective-permute-done((bf16[1,16,32,1536]{3,2,1,0:T(8,128)(2,1)}, bf16[1,16,32,1536]{3,2,1,0:T(8,128)(2,1)S(1)}, u32[]{:S(2)}, u32[]{:S(2)}) %collective-permute-start) | collective-permute-done | bytes 1572896 | tf_op jit(solution)/shard_map/ppermute | solution.py:10
  47.1 0.2 broadcast_select_fusion
  47.3 0.1 collective-permute-start.1
  47.4 37.4 %collective-permute-done.1 = bf16[1,16,32,1536]{3,2,1,0:T(8,128)(2,1)} collective-permute-done((bf16[1,16,32,1536]{3,2,1,0:T(8,128)(2,1)S(1)}, bf16[1,16,32,1536]{3,2,1,0:T(8,128)(2,1)}, u32[]{:S(2)}, u32[]{:S(2)}) %collective-permute-start.1) | collective-permute-done | bytes 1572896 | tf_op jit(solution)/shard_map/ppermute | solution.py:10
  84.9 0.2 broadcast_select_fusion.1
  85.0 0.1 collective-permute-start.2
  85.1 67.4 %collective-permute-done.2 = bf16[1,16,32,1536]{3,2,1,0:T(8,128)(2,1)S(1)} collective-permute-done((bf16[1,16,32,1536]{3,2,1,0:T(8,128)(2,1)S(1)}, bf16[1,16,32,1536]{3,2,1,0:T(8,128)(2,1)S(1)}, u32[]{:S(2)}, u32[]{:S(2)}) %collective-permute-start.2) | collective-permute-done | bytes 1572896 | tf_op jit(solution)/shard_map/ppermute | solution.py:10
  152.6 1.3 broadcast_select_fusion.2
  153.9 0.0 all-gather.2.cloned.1.call-update
  153.9 0.0 all-reduce.2.cloned.1.call-start
  153.9 44.2 %all-gather.2.cloned.1.call-done = bf16[1,16,128,1536]{3,2,1,0:T(8,128)(2,1)} async-done(((bf16[1,16,32,1536]{3,2,1,0:T(8,128)(2,1)}), bf16[1,16,128,1536]{3,2,1,0:T(8,128)(2,1)}) %all-gather.2.cloned.1.call-update) | async-done | bytes 6291472 | tf_op jit(solution)/shard_map/all_gather | solution.py:24
  198.2 11.4 %fusion.11 = bf16[4,1536,256]{1,2,0:T(8,128)(2,1)} fusion(bf16[4,1,16,128,256]{4,3,2,1,0:T(8,128)(2,1)} %param.7, bf16[1,16,128,1536]{3,2,1,0:T(8,128)(2,1)} %all-gather.2.cloned.1.call-done), kind=kOutput, calls=%fused_computation.9 | convolution fusion | flops 6444023808 | bytes 13631488 | tf_op jit(solution)/shard_map/iap,riaj->rpj/dot_general | solution.py:22
  209.5 0.0 copy-start.2
  209.5 0.0 all-reduce.2.cloned.1.call-update
  209.5 0.6 copy-done.2
  210.2 1.5 collective-permute-start.3
  211.7 4.8 %collective-permute-done.3 = bf16[1,128]{1,0:T(2,128)(2,1)S(1)} collective-permute-done((bf16[1,128]{1,0:T(2,128)(2,1)S(1)}, bf16[1,128]{1,0:T(2,128)(2,1)S(1)}, u32[]{:S(2)}, u32[]{:S(2)}) %collective-permute-start.3) | collective-permute-done | bytes 288 | tf_op jit(solution)/shard_map/ppermute | solution.py:10
  216.4 0.0 collective-permute-start.4
  216.4 5.4 %collective-permute-done.4 = bf16[1,128]{1,0:T(2,128)(2,1)S(1)} collective-permute-done((bf16[1,128]{1,0:T(2,128)(2,1)S(1)}, bf16[1,128]{1,0:T(2,128)(2,1)S(1)}, u32[]{:S(2)}, u32[]{:S(2)}) %collective-permute-start.4) | collective-permute-done | bytes 288 | tf_op jit(solution)/shard_map/ppermute | solution.py:10
  221.8 0.0 copy-start.1
  221.8 0.0 copy-start
  221.8 0.1 collective-permute-start.5
  221.9 6.2 %copy.7 = bf16[4,1,16,128,256]{3,4,2,0,1:T(8,128)(2,1)} copy(bf16[4,1,16,128,256]{4,3,2,1,0:T(8,128)(2,1)} %param.7) | data formatting | bytes 8388608 | tf_op args[1]
  228.1 0.0 collective-permute-done.5
  228.1 0.0 copy-done.1
  228.1 0.1 broadcast_subtract_fusion
  228.2 0.0 copy-done
  228.2 0.3 broadcast_add_fusion
  228.5 110.1 %all-reduce.2.cloned.1.call-done = bf16[4,1536,256]{1,2,0:T(8,128)(2,1)} async-done(((bf16[4,1536,256]{1,2,0:T(8,128)(2,1)}), bf16[4,1536,256]{1,2,0:T(8,128)(2,1)}) %all-reduce.2.cloned.1.call-update) | async-done | bytes 3145744 | tf_op jit(solution)/shard_map/psum | solution.py:28
  338.6 12.0 %fusion.5 = bf16[4,1,16,128,256]{3,4,2,0,1:T(8,128)(2,1)} fusion(bf16[4,1,16,128,256]{3,4,2,0,1:T(8,128)(2,1)} %copy.7, f32[16,128,256]{1,2,0:T(8,128)S(1)} %broadcast_add_fusion, bf16[1,16,128,1536]{3,2,1,0:T(8,128)(2,1)} %all-gather.2.cloned.1.call-done, bf16[4,1536,256]{1,2,0:T(8,128)(2,1)} %all-reduce.2.cloned.1.call-done), kind=kOutput, calls=%fused_computation.7 | convolution fusion | flops 6450839552 | bytes 19922944 | tf_op jit(solution)/shard_map/iap,rpj->riaj/dot_general | solution.py:29
  350.6 6.2 %copy.8 = bf16[4,1,16,128,256]{4,3,2,1,0:T(8,128)(2,1)} copy(bf16[4,1,16,128,256]{3,4,2,0,1:T(8,128)(2,1)} %fusion.5) | data formatting | bytes 8388608 | tf_op jit(solution)/shard_map/broadcast_in_dim | solution.py:41
  (3 shorter events, 0.0 us)
Async XLA Ops:
  6.5 191.6 %all-gather.2.cloned.1.call-start = ((), (), s32[]{:S(2)}) async-start(), calls=%async_computation | async-start | bytes 7864320 | tf_op jit(solution)/shard_map/all_gather | solution.py:24
  6.5 40.6 %collective-permute-start = (bf16[1,16,32,1536]{3,2,1,0:T(8,128)(2,1)}, bf16[1,16,32,1536]{3,2,1,0:T(8,128)(2,1)S(1)}, u32[]{:S(2)}, u32[]{:S(2)}) collective-permute-start(bf16[1,16,32,1536]{3,2,1,0:T(8,128)(2,1)} %param.6), channel_id=1, source_target_pairs={{28,0},{0,4},{4,8},{8,12},{12,16},{16,20},{20,24},{24,28},{29,1},{... | collective-permute-start | bytes 4718600 | tf_op jit(solution)/shard_map/ppermute | solution.py:10
  47.3 37.5 %collective-permute-start.1 = (bf16[1,16,32,1536]{3,2,1,0:T(8,128)(2,1)S(1)}, bf16[1,16,32,1536]{3,2,1,0:T(8,128)(2,1)}, u32[]{:S(2)}, u32[]{:S(2)}) collective-permute-start(bf16[1,16,32,1536]{3,2,1,0:T(8,128)(2,1)S(1)} %broadcast_select_fusion), channel_id=1, source_target_pairs={{24,0},{28,4},{0,8},{4,12},{8,16},{12,20},{16,24},{20,28},{25,1},{... | collective-permute-start | bytes 4718600 | tf_op jit(solution)/shard_map/ppermute | solution.py:10
  85.0 67.5 %collective-permute-start.2 = (bf16[1,16,32,1536]{3,2,1,0:T(8,128)(2,1)S(1)}, bf16[1,16,32,1536]{3,2,1,0:T(8,128)(2,1)S(1)}, u32[]{:S(2)}, u32[]{:S(2)}) collective-permute-start(bf16[1,16,32,1536]{3,2,1,0:T(8,128)(2,1)S(1)} %broadcast_select_fusion.1), channel_id=1, source_target_pairs={{16,0},{20,4},{24,8},{28,12},{0,16},{4,20},{8,24},{12,28},{17,1},{... | collective-permute-start | bytes 4718600 | tf_op jit(solution)/shard_map/ppermute | solution.py:10
  153.9 184.7 %all-reduce.2.cloned.1.call-start = ((), (), s32[]{:S(2)}) async-start(), calls=%async_computation.1 | async-start | bytes 6291456 | tf_op jit(solution)/shard_map/psum | solution.py:28
  209.5 0.7 copy-start.2
  210.2 6.2 %collective-permute-start.3 = (bf16[1,128]{1,0:T(2,128)(2,1)S(1)}, bf16[1,128]{1,0:T(2,128)(2,1)S(1)}, u32[]{:S(2)}, u32[]{:S(2)}) collective-permute-start(bf16[1,128]{1,0:T(2,128)(2,1)S(1)} %copy-done.2), channel_id=1, source_target_pairs={{28,0},{0,4},{4,8},{8,12},{12,16},{16,20},{20,24},{24,28},{29,1},{... | collective-permute-start | bytes 776 | tf_op jit(solution)/shard_map/ppermute | solution.py:10
  216.4 5.4 %collective-permute-start.4 = (bf16[1,128]{1,0:T(2,128)(2,1)S(1)}, bf16[1,128]{1,0:T(2,128)(2,1)S(1)}, u32[]{:S(2)}, u32[]{:S(2)}) collective-permute-start(bf16[1,128]{1,0:T(2,128)(2,1)S(1)} %broadcast_select_fusion.3), channel_id=1, source_target_pairs={{24,0},{28,4},{0,8},{4,12},{8,16},{12,20},{16,24},{20,28},{25,1},{... | collective-permute-start | bytes 776 | tf_op jit(solution)/shard_map/ppermute | solution.py:10
  221.8 6.3 %copy-start.1 = (f32[1,16]{1,0:T(1,128)S(1)}, f32[1,16]{1,0:T(1,128)}, u32[]{:S(2)}) copy-start(f32[1,16]{1,0:T(1,128)} %param.8) | copy-start | bytes 196
  221.8 6.4 %copy-start = (f32[256]{0:T(256)S(1)}, f32[256]{0:T(256)}, u32[]{:S(2)}) copy-start(f32[256]{0:T(256)} %param.10) | copy-start | bytes 3076
  221.8 6.3 %collective-permute-start.5 = (bf16[1,128]{1,0:T(2,128)(2,1)S(1)}, bf16[1,128]{1,0:T(2,128)(2,1)S(1)}, u32[]{:S(2)}, u32[]{:S(2)}) collective-permute-start(bf16[1,128]{1,0:T(2,128)(2,1)S(1)} %broadcast_select_fusion.4), channel_id=1, source_target_pairs={{16,0},{20,4},{24,8},{28,12},{0,16},{4,20},{8,24},{12,28},{17,1},{... | collective-permute-start | bytes 776 | tf_op jit(solution)/shard_map/ppermute | solution.py:10
Sparse Core Ops, SparseCore 0:
  154.0 44.0 all-gather.1
  209.7 128.9 all-reduce.1
where the time goes:
time: 365 us; the launch traced here: 364 us
  waiting for transfers between devices  306 us (84%)
  matrix products  23.4 us (6%)
  between operations  14.2 us (4%)
  local copies, waits for them, and re-layouts  13 us (4%)
  starting transfers between devices  4.69 us (1%)
    ppermute x6, waiting for transfers between devices, from_behind(): return lax.ppermute(block, axis, route)  152 us
    psum x1, waiting for transfers between devices, shards(): cycle_total = lax.psum(cycle_terms.astype(jnp.bfloat16), 'kocc')  110 us
    all_gather x1, waiting for transfers between devices, shards(): lax.all_gather(shifted, 'vrow', axis=2, tiled=True)[0]  44.2 us
    dot_general x1, matrix products, shards(): jnp.einsum('iap,rpj->riaj', lax.all_gather(shifted, 'vrow', axis=2, tiled...  12 us
    dot_general x1, matrix products, shards(): jnp.einsum('iap,riaj->rpj', lax.all_gather(shifted, 'vrow', axis=2, tiled...  11.4 us
  transfers between devices with their start and end apart: 8, of which 7 were waited for; matrix products, arithmetic and copies ran while one was open for 2% of the time, Pallas kernels for 0%

commit v1 on v0

v1 whole, which is shorter than its diff:
```python
import functools

import jax
import jax.numpy as jnp
from jax import lax
from jax.experimental import pallas as pl
from jax.experimental.pallas import tpu as pltpu
from jax.sharding import PartitionSpec as P

MESH = pl.DeviceIdType.MESH


def kernel(nk, nv, n, fac, amp, row_gap, col_gap, out,
           held, amp_t, acc, part, from_y, sum_y, from_z, full,
           own_sem, gx_s, gx_r, gc_s, gc_r, gf_s, gf_r,
           ry_s, ry_r, rz_s, rz_r, az_s, az_r, ay_s, ay_r):
    nx, nz = nv // 2, nk // 2
    k, v = lax.axis_index("kocc"), lax.axis_index("vrow")
    y, z = lax.rem(k, 2), k // 2
    core, x = lax.rem(v, 2), v // 2
    width = held.shape[-1]
    roots, rows, cols = amp.shape
    half = part.shape[1] // 2
    piece = half // nz

    def at_vrow(target):
        return {"kocc": k, "vrow": target}

    def at_kocc(target):
        return {"kocc": target, "vrow": v}

    mate = at_vrow(x * 2 + 1 - core)
    y_mate = at_kocc(z * 2 + 1 - y)

    def x_to(t):
        return lax.rem(x + t, nx)

    def x_from(t):
        return lax.rem(x + nx - t, nx)

    def z_to(t):
        return lax.rem(z + t, nz)

    def z_from(t):
        return lax.rem(z + nz - t, nz)

    barrier = pltpu.get_barrier_semaphore()
    partners = [mate, y_mate]
    partners += [at_vrow(x_to(t) * 2 + core) for t in range(1, nx)]
    partners += [at_kocc(z_to(t) * 2 + y) for t in range(1, nz)]
    for partner in partners:
        pl.semaphore_signal(barrier, inc=1, device_id=partner, device_id_type=MESH)
    pl.semaphore_wait(barrier, len(partners))

    def remote(src, dst, send, recv, device):
        return pltpu.make_async_remote_copy(
            src_ref=src, dst_ref=dst, send_sem=send, recv_sem=recv,
            device_id=device, device_id_type=MESH)

    def mine(p):
        return fac.at[:, :, pl.ds(pl.multiple_of(p * width, width), width)]

    def own(p):
        return pltpu.make_async_copy(mine(p), held.at[p, :, v], own_sem.at[p])

    def gather_x(p, t):
        return remote(mine(p), held.at[p, :, v], gx_s.at[p, t - 1], gx_r.at[p, t - 1],
                      at_vrow(x_to(t) * 2 + core))

    def gather_core(p):
        return remote(mine(p), held.at[p, :, v], gc_s.at[p], gc_r.at[p], mate)

    def gather_forward(p, t):
        slot = held.at[p, :, x_from(t) * 2 + core]
        return remote(slot, slot, gf_s.at[p, t - 1], gf_r.at[p, t - 1], mate)

    def reduce_y(p):
        return remote(part.at[p, pl.ds((1 - y) * half, half)], from_y.at[p],
                      ry_s.at[p], ry_r.at[p], y_mate)

    def reduce_z(p, t):
        return remote(sum_y.at[p, pl.ds(z_to(t) * piece, piece)], from_z.at[p, t - 1],
                      rz_s.at[p, t - 1], rz_r.at[p, t - 1], at_kocc(z_to(t) * 2 + y))

    def gather_z(p, t):
        where = pl.ds(y * half + z * piece, piece)
        return remote(full.at[p, where], full.at[p, where],
                      az_s.at[p, t - 1], az_r.at[p, t - 1], at_kocc(z_to(t) * 2 + y))

    def gather_y(p):
        where = pl.ds(y * half, half)
        return remote(full.at[p, where], full.at[p, where], ay_s.at[p], ay_r.at[p], y_mate)

    def start_gather(p):
        for t in range(1, nx):
            gather_x(p, t).start()
        gather_core(p).start()
        own(p).start()

    def forward(p):
        for t in range(1, nx):
            gather_x(p, t).wait_recv()
            gather_forward(p, t).start()

    start_gather(0)
    start_gather(1)

    block = 256

    @pl.loop(0, roots * (rows // block))
    def _(i):
        r, b = i // (rows // block), lax.rem(i, rows // block)
        at = pl.ds(pl.multiple_of(b * block, block), block)
        tile = amp[r, at, :]
        amp_t[r, :, at] = tile.T
        gap = row_gap[at, :] + col_gap[...]
        acc[r, at, :] = gap * tile.astype(jnp.float32)

    forward(0)

    def step(s, carry):
        @pl.when(s + 2 < n)
        def _():
            start_gather(s + 2)

        @pl.when(s + 1 < n)
        def _():
            forward(s + 1)

        @pl.when(s < n)
        def _():
            own(s).wait()
            gather_core(s).wait_recv()
            for t in range(1, nx):
                gather_forward(s, t).wait_recv()

            @pl.loop(0, roots)
            def _(r):
                dot = jnp.dot(amp_t[r], held[s].reshape(rows, width),
                              preferred_element_type=jnp.float32)
                at = pl.ds(pl.multiple_of(r * cols, cols), cols)
                part[s, at, :] = dot.astype(part.dtype)
            reduce_y(s).start()

        p1 = s - 1

        @pl.when((p1 >= 0) & (p1 < n))
        def _():
            reduce_y(p1).wait_recv()

            @pl.loop(0, nz)
            def _(i):
                at = pl.ds(pl.multiple_of(i * piece, piece), piece)
                mine_at = pl.ds(pl.multiple_of(y * half + i * piece, piece), piece)
                total = part[p1, mine_at, :].astype(jnp.float32) + from_y[p1, at, :].astype(jnp.float32)
                sum_y[p1, at, :] = total.astype(sum_y.dtype)
            for t in range(1, nz):
                reduce_z(p1, t).start()

        p2 = s - 2

        @pl.when((p2 >= 0) & (p2 < n))
        def _():
            total = sum_y[p2, pl.ds(pl.multiple_of(z * piece, piece), piece), :].astype(jnp.float32)
            for t in range(1, nz):
                reduce_z(p2, t).wait_recv()
                total += from_z[p2, t - 1].astype(jnp.float32)
            full[p2, pl.ds(pl.multiple_of(y * half + z * piece, piece), piece), :] = total.astype(full.dtype)
            for t in range(1, nz):
                gather_z(p2, t).start()

        p3 = s - 3

        @pl.when((p3 >= 0) & (p3 < n))
        def _():
            for t in range(1, nz):
                gather_z(p3, t).wait_recv()
            gather_y(p3).start()

        p4 = s - 4

        @pl.when((p4 >= 0) & (p4 < n))
        def _():
            gather_y(p4).wait_recv()

            @pl.loop(0, roots)
            def _(r):
                at = pl.ds(pl.multiple_of(r * cols, cols), cols)
                acc[r] += lax.dot_general(
                    held[p4].reshape(rows, width), full[p4, at, :],
                    (((1,), (1,)), ((), ())), preferred_element_type=jnp.float32)

        return carry

    lax.fori_loop(0, n + 4, step, 0)

    @pl.loop(0, roots * (rows // block))
    def _(i):
        r, b = i // (rows // block), lax.rem(i, rows // block)
        at = pl.ds(pl.multiple_of(b * block, block), block)
        out[r, at, :] = acc[r, at, :].astype(out.dtype)

    def drain(p, carry):
        for t in range(1, nx):
            gather_x(p, t).wait_send()
            gather_forward(p, t).wait_send()
        gather_core(p).wait_send()
        reduce_y(p).wait_send()
        for t in range(1, nz):
            reduce_z(p, t).wait_send()
            gather_z(p, t).wait_send()
        gather_y(p).wait_send()
        return carry

    lax.fori_loop(0, n, drain, 0)


def chunk_width(aux):
    for width in (256, 128):
        if aux % width == 0:
            return width
    return aux


def combine(fac, amp, row_gap, col_gap):
    nk, nv = lax.axis_size("kocc"), lax.axis_size("vrow")
    outer, inner, aux = fac.shape
    roots, rows, cols = amp.shape
    width = chunk_width(aux)
    n = aux // width
    nx, nz = nv // 2, nk // 2
    half = roots * cols // 2
    dma = pltpu.SemaphoreType.DMA
    vmem = pl.BlockSpec(memory_space=pltpu.VMEM)
    bf = jnp.bfloat16
    return pl.pallas_call(
        functools.partial(kernel, nk, nv, n),
        out_shape=jax.ShapeDtypeStruct((roots, rows, cols), bf),
        in_specs=[pl.BlockSpec(memory_space=pl.ANY), vmem, vmem, vmem],
        out_specs=vmem,
        scratch_shapes=[
            pltpu.VMEM((n, outer, nv, inner, width), bf),
            pltpu.VMEM((roots, cols, rows), bf),
            pltpu.VMEM((roots, rows, cols), jnp.float32),
            pltpu.VMEM((n, 2 * half, width), bf),
            pltpu.VMEM((n, half, width), bf),
            pltpu.VMEM((n, half, width), bf),
            pltpu.VMEM((n, nz - 1, half // nz, width), bf),
            pltpu.VMEM((n, 2 * half, width), bf),
            dma((n,)),
            dma((n, nx - 1)), dma((n, nx - 1)),
            dma((n,)), dma((n,)),
            dma((n, nx - 1)), dma((n, nx - 1)),
            dma((n,)), dma((n,)),
            dma((n, nz - 1)), dma((n, nz - 1)),
            dma((n, nz - 1)), dma((n, nz - 1)),
            dma((n,)), dma((n,)),
        ],
        compiler_params=pltpu.CompilerParams(
            collective_id=0, has_side_effects=True, vmem_limit_bytes=60 * 1024 * 1024),
        cost_estimate=pl.CostEstimate(
            flops=4 * roots * rows * cols * aux,
            bytes_accessed=4 * roots * rows * cols + 2 * outer * inner * aux,
            transcendentals=0),
    )(fac, amp, row_gap, col_gap)


def shift(distance, nk, block):
    if distance == 0:
        return block
    return lax.ppermute(block, "kocc", [(i, (i + distance) % nk) for i in range(nk)])


def shards(factors, amps, eps_occ, eps_vir, col_energy, q_index):
    nk, nv = lax.axis_size("kocc"), lax.axis_size("vrow")
    shifted, vir_shift = lax.switch(
        q_index[0], [functools.partial(shift, d, nk) for d in range(nk)], (factors, eps_vir))
    fac = shifted[0]
    occ, share, aux = fac.shape
    amp = amps[:, 0]
    roots, _, vir, cols = amp.shape
    gap = vir_shift[0].astype(jnp.float32)[None, :] - eps_occ[0][:, None]
    natural = share % 16 == 0
    if not natural:
        fac = fac.reshape(1, occ * share, aux)
        amp = amp.reshape(roots, occ, nv, share, cols).swapaxes(1, 2)
        gap = gap.reshape(occ, nv, share).swapaxes(0, 1)
    out = combine(fac, amp.reshape(roots, occ * vir, cols), gap.reshape(occ * vir, 1), col_energy[None, :])
    if not natural:
        out = out.reshape(roots, nv, occ, share, cols).swapaxes(1, 2)
    return out.reshape(roots, 1, occ, vir, cols)


def solution(mesh):
    in_specs = (
        P("kocc", None, "vrow", None),
        P(None, "kocc", None, None, "vrow"),
        P("kocc", None),
        P("kocc", None),
        P("vrow"),
        P(),
    )
    out_specs = P(None, "kocc", None, None, "vrow")
    return jax.shard_map(shards, mesh=mesh, in_specs=in_specs, out_specs=out_specs, check_vma=False)
```

time: 365 us -> 188 us (0.52)
  waiting for transfers between devices: 306 us -> 33.3 us
  Pallas kernels: 0 us -> 140 us
  matrix products: 23.4 us -> 0 us
  between operations: 14.2 us -> 0.81 us
  local copies, waits for them, and re-layouts: 13 us -> 6.81 us
    pallas_call x0 -> x1, Pallas kernels: none -> 140 us  [combine(): pl.pallas_call(functools.partial(kernel, nk, nv, n), out_shape=jax.ShapeD...]
    ppermute x6 -> x2, waiting for transfers between devices: 152 us -> 33.3 us  [shift(): lax.ppermute(block, 'kocc', [(i, (i + distance) % nk) for i in range(nk)])]
    psum x1 -> x0, waiting for transfers between devices: 110 us -> none  [shards(): cycle_total = lax.psum(cycle_terms.astype(jnp.bfloat16), 'kocc')]
    all_gather x1 -> x0, waiting for transfers between devices: 44.2 us -> none  [shards(): lax.all_gather(shifted, 'vrow', axis=2, tiled=True)[0]]
    dot_general x2 -> x0, matrix products: 23.4 us -> none  [the longest x1 12 us: shards(): jnp.einsum('iap,rpj->riaj', lax.all_gather(shifted, 'vrow', axis=2, tiled...]
    broadcast_in_dim x1 -> x0, local copies, waits for them, and re-layouts: 6.19 us -> none  [shards(): return sigma_out[:, None]]
  transfers between devices with their start and end apart: 8 -> 2, of which waited for: 7 -> 1; matrix products, arithmetic and copies ran while one was open for 2% -> 0% of each run, Pallas kernels for 0% -> 0%
where the time goes in v1:
time: 188 us; the launch traced here: 187 us
  Pallas kernels  140 us (74%)
  waiting for transfers between devices  33.3 us (18%)
  local copies, waits for them, and re-layouts  6.81 us (4%)
  starting transfers between devices  5.38 us (3%)
    pallas_call x1, Pallas kernels, combine(): pl.pallas_call(functools.partial(kernel, nk, nv, n), out_shape=jax.ShapeD...  140 us
    ppermute x2, waiting for transfers between devices, shift(): lax.ppermute(block, 'kocc', [(i, (i + distance) % nk) for i in range(nk)])  33.3 us
    ppermute x2, starting transfers between devices, shift(): lax.ppermute(block, 'kocc', [(i, (i + distance) % nk) for i in range(nk)])  5.38 us
    unnamed x7, local copies, waits for them, and re-layouts  5.36 us
  transfers between devices with their start and end apart: 2, of which 1 were waited for; matrix products, arithmetic and copies ran while one was open for 0% of the time, Pallas kernels for 0%

profile of v1, /device:TPU:0, one launch (start us, length us, event | category | flops | bytes accessed | tf_op | source)
XLA Modules:
  0.0 186.8 jit_solution(5200518249152265711)
XLA Ops:
  0.0 0.0 copy-start
  0.0 0.0 copy-start.2
  0.8 0.6 copy-done
  1.4 0.0 copy-done.2
  1.4 0.0 copy-start.1
  1.4 38.8 %conditional.1 = ((bf16[1,128]{1,0:T(2,128)(2,1)S(1)}, bf16[1,16,32,1536]{3,2,1,0:T(8,128)(2,1)S(1)})) conditional(s32[]{:T(128)} %bitcast, (bf16[1,128]{1,0:T(2,128)(2,1)S(1)}, bf16[1,16,32,1536]{3,2,1,0:T(8,128)(2,1)S(1)}) %tuple.95, (bf16[1,128]{1,0:T(2,128)(2,1)S(1)}, ...), branch_computations={%region_0.0_spmd, %region_1.0_spmd, %region_2.0_spmd, %region_3.0_... | conditional | bytes 9438824 | solution.py:276
  1.4 5.0 %collective-permute-start.9 = (bf16[1,16,32,1536]{3,2,1,0:T(8,128)(2,1)S(1)}, bf16[1,16,32,1536]{3,2,1,0:T(8,128)(2,1)S(1)}, u32[]{:S(2)}, u32[]{:S(2)}) collective-permute-start(bf16[1,16,32,1536]{3,2,1,0:T(8,128)(2,1)S(1)} %get-tuple-element.51), channel_id=1, source_target_pairs={{0,20},{4,24},{8,28},{12,0},{16,4},{20,8},{24,12},{28,16},{1,21},{... | collective-permute-start | bytes 4718600 | tf_op jit(solution)/shard_map/cond/branch_5_fun/ppermute | solution.py:271
  6.4 0.4 collective-permute-start.8
  6.8 33.3 %collective-permute-done.8 = bf16[1,128]{1,0:T(2,128)(2,1)S(1)} collective-permute-done((bf16[1,128]{1,0:T(2,128)(2,1)S(1)}, bf16[1,128]{1,0:T(2,128)(2,1)S(1)}, u32[]{:S(2)}, u32[]{:S(2)}) %collective-permute-start.8) | collective-permute-done | bytes 288 | tf_op jit(solution)/shard_map/cond/branch_5_fun/ppermute | solution.py:271
  40.2 0.0 collective-permute-done.9
  40.2 0.1 copy.21
  40.3 0.0 copy-done.1
  40.3 0.1 broadcast_subtract_fusion
  40.4 1.4 copy.8.row_gap
  41.7 140.4 %shard_map.64 = bf16[4,2048,256]{2,1,0:T(8,128)(2,1)} custom-call(bf16[16,32,1536]{2,1,0:T(8,128)(2,1)S(1)} %bitcast.13, bf16[4,2048,256]{2,1,0:T(8,128)(2,1)} %bitcast.16, f32[2048,1]{1,0:T(8,128)} %copy.8.row_gap, f32[1,256]{1,0:T(1,128)} %bitcast.17), custom_call_target="tpu_custom_call" | custom-call | flops 12884901888 | bytes 9961472 | tf_op jit(solution)/shard_map/pallas_call | solution.py:236
  182.1 4.7 %copy.32 = bf16[4,1,16,128,256]{4,3,2,1,0:T(8,128)(2,1)} copy(bf16[4,1,16,128,256]{4,3,2,1,0:T(8,128)(2,1)} %bitcast.12) | data formatting | bytes 8388608
  (2 shorter events, 0.0 us)
Async XLA Ops:
  0.0 1.4 copy-start
  0.0 1.4 copy-start.2
  1.4 38.9 %copy-start.1 = (f32[1,16]{1,0:T(1,128)S(1)}, f32[1,16]{1,0:T(1,128)}, u32[]{:S(2)}) copy-start(f32[1,16]{1,0:T(1,128)} %param.16) | copy-start | bytes 196
  1.4 38.7 %collective-permute-start.9 = (bf16[1,16,32,1536]{3,2,1,0:T(8,128)(2,1)S(1)}, bf16[1,16,32,1536]{3,2,1,0:T(8,128)(2,1)S(1)}, u32[]{:S(2)}, u32[]{:S(2)}) collective-permute-start(bf16[1,16,32,1536]{3,2,1,0:T(8,128)(2,1)S(1)} %get-tuple-element.51), channel_id=1, source_target_pairs={{0,20},{4,24},{8,28},{12,0},{16,4},{20,8},{24,12},{28,16},{1,21},{... | collective-permute-start | bytes 4718600 | tf_op jit(solution)/shard_map/cond/branch_5_fun/ppermute | solution.py:271
  6.4 33.7 %collective-permute-start.8 = (bf16[1,128]{1,0:T(2,128)(2,1)S(1)}, bf16[1,128]{1,0:T(2,128)(2,1)S(1)}, u32[]{:S(2)}, u32[]{:S(2)}) collective-permute-start(bf16[1,128]{1,0:T(2,128)(2,1)S(1)} %get-tuple-element.50), channel_id=1, source_target_pairs={{0,20},{4,24},{8,28},{12,0},{16,4},{20,8},{24,12},{28,16},{1,21},{... | collective-permute-start | bytes 776 | tf_op jit(solution)/shard_map/cond/branch_5_fun/ppermute | solution.py:271
